TPU v7x, 256 devices: a whole 4x4x8 slice. The times are simulated.
256 devices in a mesh: rep: 32 (over z, y), fsdp: 8 (over x, core).
Axes of the slice: x: 4, y: 4, z: 8, core: 2. Of those that a mesh axis runs over, the one named last changes fastest.
Arguments:
- tokens: bfloat16 [131072, 4096], P(('rep', 'fsdp')), may hold values from -6 to 6
- cotangent: bfloat16 [131072, 512], P(('rep', 'fsdp')), may hold values from -6 to 6
- inner_params: bfloat16 [32, 4096, 512], P('rep', 'fsdp'), may hold values from -6 to 6
- first_moment: float32 [32, 4096, 512], P('rep', 'fsdp'), may hold values from -2 to 2
- second_moment: float32 [32, 4096, 512], P('rep', 'fsdp'), may hold values from 0.01 to 1
- anchor: float32 [4096, 512], P('fsdp'), may hold values from -6 to 6
- feedback: float32 [32, 4096, 512], P('rep', 'fsdp'), may hold values from -4 to 4
- momentum: float32 [4096, 512], P('fsdp'), may hold values from -4 to 4
- sel_blocks: int32 [32, 8, 256], P('rep', 'fsdp'), may hold values from 0 to 1023, as said below
- sel_count: int32 [32, 8], P('rep', 'fsdp'), may hold values from 64 to 256
Outputs:
- key_out: bfloat16 [131072, 512], P(('rep', 'fsdp'))
- anchor_new: float32 [4096, 512], P('fsdp')
- feedback_new: float32 [32, 4096, 512], P('rep', 'fsdp')
- momentum_new: float32 [4096, 512], P('fsdp')
Inputs may be any that keep to these rules, and one draw needn't show every extreme that they name: `sel_blocks`: the first sel_count[r, f] entries of list (r, f) are distinct blocks of the shard's 1024; the entries past them are other blocks of the shard, not selected. Owner o's range is blocks o * 32 up to (o + 1) * 32; at most 16 selected blocks of one list lie in one owner's range. For each fsdp index, one owner's range holds exactly 16 selected blocks of every list.
All inputs are finite; a program needn't handle non-finite values.
Results may differ from a plain program's by a relative error of at most 0.004.
Values may be sent and summed in bfloat16 or wider, within the bound.
A program may use at most 128 MiB of HBM per device.

v0:
```python
import math

import jax
import jax.numpy as jnp
from jax import lax
from jax.sharding import PartitionSpec as P

D = 4096
BLK = 256


beta_first = 0.9
beta_second = 0.95
epsilon = 1e-08
decay_rate = 0.1
inner_rate = 1.0
outer_rate = 0.7
outer_momentum = 0.9


def shards(
    tokens,
    cotangent,
    inner_params,
    first_moment,
    second_moment,
    anchor,
    feedback,
    momentum,
    sel_blocks,
    sel_count,
):
    weights = inner_params[0]
    shard_rows, columns = weights.shape
    inverse = 1.0 / math.sqrt(D)
    inputs = tokens
    key_sum = jnp.dot(
        inputs,
        lax.all_gather(weights, "fsdp", axis=0, tiled=True),
        preferred_element_type=jnp.float32,
    )
    key_out = (key_sum * inverse).astype(jnp.bfloat16)
    inputs = tokens
    gradient = lax.psum_scatter(
        (
            lax.dot_general(
                inputs, cotangent, (((0,), (0,)), ((), ())), preferred_element_type=jnp.float32
            )
            * inverse
        ).astype(jnp.bfloat16),
        "fsdp",
        scatter_dimension=0,
        tiled=True,
    ).astype(jnp.float32)
    first_new = beta_first * first_moment[0] + (1.0 - beta_first) * gradient
    second_new = beta_second * second_moment[0] + (1.0 - beta_second) * gradient * gradient
    master = weights.astype(jnp.float32)
    stepped = master - inner_rate * (
        first_new / (jnp.sqrt(second_new) + epsilon) + decay_rate * master
    )
    combined = feedback[0] + (anchor - stepped)
    per_row = columns // BLK
    block_count = shard_rows * per_row
    block_view = combined.reshape(block_count, BLK)
    chosen = sel_blocks.reshape(-1)
    amount = sel_count.reshape(())
    positions = jnp.arange(chosen.shape[0], dtype=jnp.int32)
    usable = positions < amount
    marked = jnp.any(
        (chosen[:, None] == jnp.arange(block_count, dtype=jnp.int32)[None, :]) & usable[:, None],
        axis=0,
    )
    picked = jnp.where(usable[:, None], block_view[chosen], 0.0)
    every_tile, every_index = (
        lax.all_gather(picked, "rep", axis=0, tiled=True),
        lax.all_gather(chosen, "rep", axis=0, tiled=True),
    )
    summed = jnp.zeros((block_count, BLK), jnp.float32).at[every_index].add(every_tile)
    average = summed.reshape(shard_rows, columns) / lax.axis_size("rep")
    momentum_new = outer_momentum * momentum + average
    anchor_new = anchor - outer_rate * (average + outer_momentum * momentum_new)
    feedback_new = jnp.where(marked[:, None], 0.0, block_view).reshape(shard_rows, columns)
    return (key_out, anchor_new, feedback_new[None], momentum_new)


def solution(mesh):
    placed = (
        P(("rep", "fsdp"), None),
        P(("rep", "fsdp"), None),
        P("rep", "fsdp", None),
        P("rep", "fsdp", None),
        P("rep", "fsdp", None),
        P("fsdp", None),
        P("rep", "fsdp", None),
        P("fsdp", None),
        P("rep", "fsdp", None),
        P("rep", "fsdp"),
    )
    return jax.shard_map(
        shards,
        mesh=mesh,
        in_specs=placed,
        out_specs=(
            P(("rep", "fsdp"), None),
            P("fsdp", None),
            P("rep", "fsdp", None),
            P("fsdp", None),
        ),
        check_vma=False,
    )
```

profile of v0, /device:TPU:1, one launch (start us, length us, event | category | flops | bytes accessed | tf_op | source)
XLA Modules:
  0.0 251.0 jit_solution(1063860447947579783)
XLA Ops:
  7.2 0.0 copy-start
  7.2 0.0 reduce-scatter.2.cloned.1.call-start
  7.2 1.0 copy-done
  8.2 6.5 %multiply_convert_fusion = bf16[4096,512]{1,0:T(8,128)(2,1)} fusion(bf16[512,4096]{1,0:T(8,128)(2,1)} %param.10, bf16[512,512]{1,0:T(8,128)(2,1)S(1)} %copy-done), kind=kOutput, calls=%fused_computation.2 | convolution fusion | flops 2151677952 | bytes 8912896 | tf_op jit(solution)/shard_map/dot_general | solution.py:46
  14.7 0.0 copy-start.3
  14.7 0.0 copy-start.1
  14.7 0.0 reduce-scatter.2.cloned.1.call-update
  14.8 0.0 all-gather.7.cloned.1.call-start
  14.8 0.7 all-gather.7.cloned.1.call-update
  15.5 0.0 all-gather.5.cloned.1.call-start
  16.2 0.0 copy-done.3
  16.2 0.2 fusion.17
  16.4 0.3 broadcast_in_dim.43
  16.7 0.1 copy.16
  16.8 0.1 broadcast_in_dim.44
  16.9 0.4 copy.17
  17.4 38.8 %reduce-scatter.2.cloned.1.call-done = bf16[512,512]{1,0:T(8,128)(2,1)} async-done(((bf16[4096,512]{1,0:T(8,128)(2,1)}), bf16[512,512]{1,0:T(8,128)(2,1)}) %reduce-scatter.2.cloned.1.call-update) | async-done | bytes 524304 | tf_op jit(solution)/shard_map/reduce_scatter | solution.py:44
  56.2 0.0 copy-done.1
  56.2 0.0 copy-done.2
  56.2 3.9 %select_bitcast_fusion = (f32[1,512,512]{2,1,0:T(8,128)}, f32[512,512]{1,0:T(8,128)S(1)}) fusion(pred[512,512]{1,0:T(8,128)(4,1)S(1)} %copy.17, f32[512,512]{1,0:T(8,128)S(1)} %copy-done.1, f32[1,512,512]{2,1,0:T(8,128)} %param.14, bf16[512,512]{1,0:T(8,128)(2,1)} %reduce-scatter.2.cloned.1.call-done, f32[1,512,512]{2,1,0:T(8,128)} %param.13, ...), kind=kLoop, calls=%fused_computation.19 | loop fusion | flops 4456448 | bytes 7602176 | tf_op jit(solution)/shard_map/jit(_where)/select_n | solution.py:82
  60.1 0.2 reshape.71
  60.3 1.0 gather_fusion
  61.2 0.8 broadcast_select_fusion
  62.1 0.0 all-gather.5.cloned.1.call-update
  62.1 36.8 %all-gather.1 = s32[1,1,8192]{2,1,0:T(1,128)S(1)} all-gather(s32[1,1,256]{2,1,0:T(1,128)S(1)} %copy-done.3), channel_id=3, replica_groups=mesh['rep'=32,'fsdp'=8] {'rep'}, dimensions={2}, use_global_device_ids=true | all-gather | bytes 33792 | tf_op jit(solution)/shard_map/all_gather | solution.py:76
  98.8 0.0 all-gather.7.cloned.1.call-done
  98.9 6.6 %fusion.5 = bf16[512,512]{1,0:T(8,128)(2,1)} fusion(bf16[512,4096]{1,0:T(8,128)(2,1)} %param.10, bf16[1,4096,512]{2,1,0:T(8,128)(2,1)} %all-gather.7.cloned.1.call-done), kind=kOutput, calls=%fused_computation.10 | convolution fusion | flops 2148007936 | bytes 8912896 | tf_op jit(solution)/shard_map/dot_general | solution.py:37
  105.5 90.5 %all-gather.5.cloned.1.call-done = f32[8192,256]{1,0:T(8,128)} async-done(((f32[256,256]{1,0:T(8,128)}), f32[8192,256]{1,0:T(8,128)}) %all-gather.5.cloned.1.call-update) | async-done | bytes 8388624 | tf_op jit(solution)/shard_map/all_gather | solution.py:75
  196.0 44.8 %scatter_custom_fusion = f32[1024,256]{1,0:T(8,128)S(1)} fusion(s32[8192]{0:T(1024)S(1)} %compare_select_fusion, f32[8192,256]{1,0:T(8,128)} %all-gather.5.cloned.1.call-done, f32[]{:T(128)} %constant.13.clone.1), kind=kCustom, calls=%fused_computation.26 | custom fusion | flops 2097152 | bytes 1049088 | tf_op jit(solution)/shard_map/scatter-add | solution.py:78
  240.8 0.1 broadcast_multiply_fusion
  240.9 0.3 div.14
  241.2 3.3 %multiply_subtract_fusion = (f32[512,512]{1,0:T(8,128)}, f32[512,512]{1,0:T(8,128)}) fusion(f32[512,512]{1,0:T(8,128)} %param.15, f32[512,512]{1,0:T(8,128)S(1)} %div.14, f32[512,512]{1,0:T(8,128)} %param.17), kind=kLoop, calls=%fused_computation.21 | loop fusion | flops 1572864 | bytes 5242880 | tf_op jit(solution)/shard_map/sub | solution.py:81
  (5 shorter events, 0.0 us)
Async XLA Ops:
  7.2 1.0 copy-start
  7.2 49.0 %reduce-scatter.2.cloned.1.call-start = ((), (), s32[]{:S(2)}) async-start(), calls=%async_computation.1 | async-start | bytes 4718592 | tf_op jit(solution)/shard_map/reduce_scatter | solution.py:44
  14.7 1.5 copy-start.3
  14.7 41.5 %copy-start.1 = (f32[512,512]{1,0:T(8,128)S(1)}, f32[512,512]{1,0:T(8,128)}, u32[]{:S(2)}) copy-start(f32[512,512]{1,0:T(8,128)} %param.15) | copy-start | bytes 3145732
  14.7 41.5 %copy-start.2 = (bf16[1,512,512]{2,1,0:T(8,128)(2,1)S(1)}, bf16[1,512,512]{2,1,0:T(8,128)(2,1)}, u32[]{:S(2)}) copy-start(bf16[1,512,512]{2,1,0:T(8,128)(2,1)} %param.12) | copy-start | bytes 1572868
  14.8 84.1 %all-gather.7.cloned.1.call-start = ((), (), s32[]{:S(2)}) async-start(), calls=%async_computation.3 | async-start | bytes 4718592 | tf_op jit(solution)/shard_map/all_gather | solution.py:39
  15.5 180.5 %all-gather.5.cloned.1.call-start = ((), (), s32[]{:S(2)}) async-start(), calls=%async_computation.2 | async-start | bytes 8650752 | tf_op jit(solution)/shard_map/all_gather | solution.py:75
Sparse Core Ops, SparseCore 0:
  14.9 41.2 reduce-scatter.1
  58.1 36.9 all-gather.6
  98.2 97.7 all-gather.4
where the time goes:
time: 251 us
  waiting for transfers between devices  130 us (52%)
  other arithmetic  53.1 us (21%)
  blocking collectives  36.8 us (15%)
  between operations  14.5 us (6%)
  matrix products  13.1 us (5%)
  local copies, waits for them, and re-layouts  3.3 us (1%)
    all_gather x1, waiting for transfers between devices, shards(): lax.all_gather(picked, 'rep', axis=0, tiled=True)  90.5 us
    scatter-add x1, other arithmetic, shards(): jnp.zeros((block_count, BLK), jnp.float32).at[every_index].add(every_tile)  44.8 us
    reduce_scatter x1, waiting for transfers between devices, shards(): lax.psum_scatter((lax.dot_general(inputs, cotangent, (((0,), (0,)), ((),...  38.8 us
    all_gather x1, blocking collectives, shards(): lax.all_gather(chosen, 'rep', axis=0, tiled=True)  36.8 us
    dot_general x1, matrix products, shards(): jnp.dot(inputs, lax.all_gather(weights, 'fsdp', axis=0, tiled=True), pref...  6.59 us
    dot_general x1, matrix products, shards(): lax.dot_general(inputs, cotangent, (((0,), (0,)), ((), ())), preferred_el...  6.52 us
  transfers between devices with their start and end apart: 3, of which 2 were waited for; matrix products, arithmetic and copies ran while one was open for 5% of the time, Pallas kernels for 0%

commit v1 on v0

v1 whole, which is shorter than its diff:
```python
import math

import jax
import jax.numpy as jnp
from jax import lax
from jax.experimental import pallas as pl
from jax.experimental.pallas import tpu as pltpu
from jax.sharding import PartitionSpec as P

D = 4096
BLK = 256
COLS = 512
ROWS = 512
TOK = 512
KSEL = 256
NX = 4
NY = 4
NZ = 8
NP = 2
W = COLS // NP
HALF = W // 2
YR = ROWS // NY
ZR = YR // NZ

beta_first = 0.9
beta_second = 0.95
epsilon = 1e-08
decay_rate = 0.1
inner_rate = 1.0
outer_rate = 0.7
outer_momentum = 0.9

MESH = pl.DeviceIdType.MESH
F32 = jnp.float32
BF16 = jnp.bfloat16

ORDER = (2, 1, 3, 0)


def kernel(
    tok_hbm, cot_hbm, par_hbm, first_hbm, second_hbm, anchor_hbm, feed_hbm, mom_hbm, sel_hbm, cnt_hbm,
    key_hbm, anchor_out, feed_out, mom_out,
    tok, cot, cot_t, wts, first, second, anchor, feed, mom, sel, cnt,
    part, sib_in, msg, fin, grad_t, mark, outg, ybuf, zsrc, zbuf, avg,
    acc, key_v, anchor_v, feed_v, mom_v,
    load_sem, store_sem,
    sib_s, sib_r, x_s, x_r, ag_s, ag_r, rel_s, rel_r,
    y_s, y_r, z_s, z_r, gz_s, gz_r, gy_s, gy_r,
):
    rep = lax.axis_index("rep")
    fs = lax.axis_index("fsdp")
    core = lax.rem(fs, 2)
    x = fs // 2
    y = lax.rem(rep, NY)
    z = rep // NY

    def on_x(k):
        return (rep, lax.rem(x + k, NX) * 2 + core)

    def on_y(k):
        return (z * NY + lax.rem(y + k, NY), fs)

    def on_z(k):
        return (lax.rem(z + k, NZ) * NY + y, fs)

    sib = (rep, x * 2 + 1 - core)

    def remote(src, dst, send, recv, dev):
        return pltpu.make_async_remote_copy(
            src_ref=src, dst_ref=dst, send_sem=send, recv_sem=recv, device_id=dev, device_id_type=MESH
        )

    loads = []

    def load(src, dst):
        c = pltpu.make_async_copy(src, dst, load_sem.at[len(loads)])
        loads.append(c)
        c.start()
        return c

    l_cot = load(cot_hbm, cot)
    l_w = load(par_hbm.at[0], wts.at[7])
    l_tok = []
    for i in range(8):
        chip = lax.rem(x + ORDER[i // 2], NX)
        shard = chip * 2 + (1 - core if i % 2 == 0 else core)
        l_tok.append(load(tok_hbm.at[:, pl.ds(pl.multiple_of(shard * ROWS, ROWS), ROWS)], tok.at[i]))
    l_sel = load(sel_hbm, sel)
    l_cnt = load(cnt_hbm, cnt)
    l_state = [
        load(first_hbm.at[0], first),
        load(second_hbm.at[0], second),
        load(anchor_hbm, anchor),
        load(feed_hbm.at[0], feed),
        load(mom_hbm, mom),
    ]

    barrier = pltpu.get_barrier_semaphore()
    peers = [sib, on_x(1), on_x(3)] + [on_y(k) for k in range(1, NY)] + [on_z(k) for k in range(1, NZ)]
    for dev in peers:
        pl.semaphore_signal(barrier, inc=1, device_id=dev, device_id_type=MESH)

    l_cot.wait()
    cot_t[...] = jnp.transpose(cot[...], (1, 0))
    l_w.wait()
    pl.semaphore_wait(barrier, len(peers))

    def ag(n, src_slot, rows, dst_slot, k):
        c = remote(
            wts.at[src_slot, pl.ds(rows, 256)], wts.at[dst_slot, pl.ds(rows, 256)], ag_s.at[n], ag_r.at[n], on_x(k)
        )
        c.start()
        return c

    ag_plus_a = ag(0, 7, 0, 5, 1)
    ag_minus_b = ag(1, 7, 256, 3, 3)

    def products(h):
        def body(i, _):
            p = lax.dot_general(
                cot_t[h * W : (h + 1) * W, :], tok[i], (((1,), (0,)), ((), ())), preferred_element_type=F32
            )
            part[h, i] = (p * (1.0 / math.sqrt(D))).astype(BF16)
            return 0

        copies = []
        for i in range(8):
            if h == 0:
                l_tok[i].wait()
            body(i, 0)
            if i % 2 == 0:
                c = remote(part.at[h, i], sib_in.at[h, i // 2], sib_s.at[h, i // 2], sib_r.at[h, i // 2], sib)
                c.start()
                copies.append(c)
        return copies

    def x_send(h, n, src, dst, k):
        c = remote(src, dst, x_s.at[h, n], x_r.at[h, n], on_x(k))
        c.start()
        return c

    def pair_sum(h, i, rows):
        return part[h, 2 * i + 1, rows : rows + HALF, :].astype(F32) + sib_in[h, i, rows : rows + HALF, :].astype(F32)

    A, B = 0, HALF

    def x_first(h, sib_c):
        sib_c[0].wait_recv()
        msg[h, 0] = pair_sum(h, 0, A).astype(BF16)
        c0 = x_send(h, 0, msg.at[h, 0], fin.at[h, 0, pl.ds(A, HALF)], 1)
        msg[h, 1] = pair_sum(h, 0, B).astype(BF16)
        c1 = x_send(h, 1, msg.at[h, 1], fin.at[h, 0, pl.ds(B, HALF)], 3)
        sib_c[1].wait_recv()
        msg[h, 2] = pair_sum(h, 1, B).astype(BF16)
        c2 = x_send(h, 2, msg.at[h, 2], fin.at[h, 1, pl.ds(B, HALF)], 1)
        sib_c[2].wait_recv()
        msg[h, 3] = pair_sum(h, 2, A).astype(BF16)
        c3 = x_send(h, 3, msg.at[h, 3], fin.at[h, 2, pl.ds(A, HALF)], 3)
        return [c0, c1, c2, c3]

    def x_second(h, c):
        c[0].wait_recv()
        msg[h, 4] = (pair_sum(h, 1, A) + fin[h, 0, A : A + HALF, :].astype(F32)).astype(BF16)
        c4 = x_send(h, 4, msg.at[h, 4], fin.at[h, 1, pl.ds(A, HALF)], 1)
        c[1].wait_recv()
        msg[h, 5] = (pair_sum(h, 2, B) + fin[h, 0, B : B + HALF, :].astype(F32)).astype(BF16)
        c5 = x_send(h, 5, msg.at[h, 5], fin.at[h, 2, pl.ds(B, HALF)], 3)
        return c + [c4, c5]

    def marks():
        l_sel.wait()
        l_cnt.wait()
        place = lax.broadcasted_iota(jnp.int32, (1, KSEL), 1)
        names = jnp.where(place < cnt[...], sel[...], -1)
        ones = jnp.ones((KSEL, W), BF16)
        for h in range(NP):
            for r in range(0, ROWS, 128):
                block = (lax.broadcasted_iota(jnp.int32, (128, KSEL), 0) + r) * NP + h
                hit = jnp.where(block == names, 1.0, 0.0).astype(BF16)
                mark[h, r : r + 128, :] = jnp.dot(hit, ones, preferred_element_type=F32)

    def store(src, dst):
        c = pltpu.make_async_copy(src, dst, store_sem.at[len(stores)])
        stores.append(c)
        c.start()

    stores = []

    def adam(h, sib_c, c):
        sib_c[3].wait_recv()
        for n in (2, 3, 4, 5):
            c[n].wait_recv()
        cols = slice(h * W, (h + 1) * W)

        for d in range(0, ROWS, 128):
            s = slice(d, d + 128)
            total = (
                part[h, 7, :, s].astype(F32) + sib_in[h, 3, :, s].astype(F32)
                + fin[h, 1, :, s].astype(F32) + fin[h, 2, :, s].astype(F32)
            )
            grad_t[s, :] = jnp.transpose(total, (1, 0))

        def body(n, _):
            s = pl.ds(pl.multiple_of(n * 32, 32), 32)
            g = grad_t[s, :]
            first_new = beta_first * first[s, cols] + (1.0 - beta_first) * g
            second_new = beta_second * second[s, cols] + (1.0 - beta_second) * g * g
            master = wts[7, s, cols].astype(F32)
            stepped = master - inner_rate * (
                first_new / (jnp.sqrt(second_new) + epsilon) + decay_rate * master
            )
            combined = feed[s, cols] + (anchor[s, cols] - stepped)
            marked = mark[h, s, :] > 0.5
            feed_v[h, s, :] = jnp.where(marked, 0.0, combined)
            outg[h, s, :] = jnp.where(marked, combined, 0.0).astype(BF16)
            return 0

        lax.fori_loop(0, ROWS // 32, body, 0)
        store(feed_v.at[h], feed_out.at[0, :, pl.ds(h * W, W)])
        copies = []
        for k in range(1, NY):
            to = lax.rem(y + k, NY)
            c = remote(
                outg.at[h, pl.ds(pl.multiple_of(to * YR, YR), YR)], ybuf.at[h, k - 1],
                y_s.at[h, k - 1], y_r.at[h, k - 1], on_y(k),
            )
            c.start()
            copies.append(c)
        return copies

    def sync_z(h, c):
        for one in c:
            one.wait_recv()
        total = outg[h, pl.ds(pl.multiple_of(y * YR, YR), YR), :].astype(F32)
        for k in range(NY - 1):
            total = total + ybuf[h, k].astype(F32)
        zsrc[h] = total.astype(BF16)
        copies = []
        for k in range(1, NZ):
            to = lax.rem(z + k, NZ)
            c = remote(
                zsrc.at[h, pl.ds(pl.multiple_of(to * ZR, ZR), ZR)], zbuf.at[h, k - 1],
                z_s.at[h, k - 1], z_r.at[h, k - 1], on_z(k),
            )
            c.start()
            copies.append(c)
        return copies

    def gather_z(h, c):
        for one in c:
            one.wait_recv()
        total = zsrc[h, pl.ds(pl.multiple_of(z * ZR, ZR), ZR), :].astype(F32)
        for k in range(NZ - 1):
            total = total + zbuf[h, k].astype(F32)
        mine = pl.ds(pl.multiple_of(y * YR + z * ZR, ZR), ZR)
        avg[h, mine, :] = (total * (1.0 / (NY * NZ))).astype(BF16)
        copies = []
        for k in range(1, NZ):
            c = remote(avg.at[h, mine], avg.at[h, mine], gz_s.at[h, k - 1], gz_r.at[h, k - 1], on_z(k))
            c.start()
            copies.append(c)
        return copies

    def gather_y(h, c):
        for one in c:
            one.wait_recv()
        mine = pl.ds(pl.multiple_of(y * YR, YR), YR)
        copies = []
        for k in range(1, NY):
            c = remote(avg.at[h, mine], avg.at[h, mine], gy_s.at[h, k - 1], gy_r.at[h, k - 1], on_y(k))
            c.start()
            copies.append(c)
        return copies

    def outer(h, c):
        for one in c:
            one.wait_recv()
        cols = slice(h * W, (h + 1) * W)

        def body(n, _):
            s = pl.ds(pl.multiple_of(n * 32, 32), 32)
            average = avg[h, s, :].astype(F32)
            momentum_new = outer_momentum * mom[s, cols] + average
            mom_v[h, s, :] = momentum_new
            anchor_v[h, s, :] = anchor[s, cols] - outer_rate * (average + outer_momentum * momentum_new)
            return 0

        lax.fori_loop(0, ROWS // 32, body, 0)
        store(mom_v.at[h], mom_out.at[:, pl.ds(h * W, W)])
        store(anchor_v.at[h], anchor_out.at[:, pl.ds(h * W, W)])

    def key_block(slot, rows, size, begin=False):
        def body(n, _):
            s = pl.ds(pl.multiple_of(n * 128, 128), 128)
            p = jnp.dot(
                tok[slot, s, rows : rows + size], wts[slot, rows : rows + size, :], preferred_element_type=F32
            )
            acc[s, :] = p if begin else acc[s, :] + p
            return 0

        lax.fori_loop(0, TOK // 128, body, 0)

    def relay(n, slot, rows, size):
        c = remote(
            wts.at[slot, pl.ds(rows, size)], wts.at[slot - 1, pl.ds(rows, size)], rel_s.at[n], rel_r.at[n], sib
        )
        c.start()
        return c

    sib0 = products(0)
    x0 = x_first(0, sib0)
    sib1 = products(1)
    x0 = x_second(0, x0)
    x1 = x_first(1, sib1)
    rel = [relay(0, 7, 0, ROWS)]
    marks()
    for one in l_state:
        one.wait()
    key_block(7, 0, ROWS, begin=True)
    y0 = adam(0, sib0, x0)
    x1 = x_second(1, x1)

    ag_plus_b = ag(2, 7, 256, 5, 1)
    ag_minus_a = ag(3, 7, 0, 3, 3)
    ag_plus_a.wait_recv()
    ag_plus_f = ag(4, 5, 0, 1, 1)
    rel.append(relay(1, 5, 0, 256))
    ag_minus_b.wait_recv()
    ag_minus_f = ag(5, 3, 256, 1, 3)
    rel.append(relay(2, 3, 256, 256))

    z0 = sync_z(0, y0)
    y1 = adam(1, sib1, x1)
    gz0 = gather_z(0, z0)
    rel[0].wait_recv()
    key_block(6, 0, ROWS)
    z1 = sync_z(1, y1)
    gy0 = gather_y(0, gz0)
    gz1 = gather_z(1, z1)
    outer(0, gy0)
    gy1 = gather_y(1, gz1)
    ag_plus_b.wait_recv()
    rel.append(relay(3, 5, 256, 256))
    ag_minus_a.wait_recv()
    rel.append(relay(4, 3, 0, 256))
    key_block(5, 0, ROWS)
    key_block(3, 0, ROWS)
    outer(1, gy1)
    ag_plus_f.wait_recv()
    rel.append(relay(5, 1, 0, 256))
    ag_minus_f.wait_recv()
    rel.append(relay(6, 1, 256, 256))
    key_block(1, 0, ROWS)
    for n in (1, 3):
        rel[n].wait_recv()
    key_block(4, 0, ROWS)
    for n in (2, 4):
        rel[n].wait_recv()
    key_block(2, 0, ROWS)
    for n in (5, 6):
        rel[n].wait_recv()
    key_block(0, 0, ROWS)
    key_v[...] = (acc[...] * (1.0 / math.sqrt(D))).astype(BF16)
    store(key_v, key_hbm)

    ags = [ag_plus_a, ag_minus_b, ag_plus_b, ag_minus_a, ag_plus_f, ag_minus_f]
    for one in sib0 + sib1 + x0 + x1 + y0 + y1 + z0 + z1 + gz0 + gz1 + gy0 + gy1 + ags + rel:
        one.wait_send()
    for one in stores:
        one.wait()


def shards(
    tokens,
    cotangent,
    inner_params,
    first_moment,
    second_moment,
    anchor,
    feedback,
    momentum,
    sel_blocks,
    sel_count,
):
    dma = pltpu.SemaphoreType.DMA
    any_space = pl.BlockSpec(memory_space=pl.ANY)
    return pl.pallas_call(
        kernel,
        out_shape=(
            jax.ShapeDtypeStruct((TOK, COLS), BF16),
            jax.ShapeDtypeStruct((ROWS, COLS), F32),
            jax.ShapeDtypeStruct((1, ROWS, COLS), F32),
            jax.ShapeDtypeStruct((ROWS, COLS), F32),
        ),
        in_specs=[any_space] * 10,
        out_specs=(any_space,) * 4,
        scratch_shapes=[
            pltpu.VMEM((8, TOK, ROWS), BF16),
            pltpu.VMEM((TOK, COLS), BF16),
            pltpu.VMEM((COLS, TOK), BF16),
            pltpu.VMEM((8, ROWS, COLS), BF16),
            pltpu.VMEM((ROWS, COLS), F32),
            pltpu.VMEM((ROWS, COLS), F32),
            pltpu.VMEM((ROWS, COLS), F32),
            pltpu.VMEM((ROWS, COLS), F32),
            pltpu.VMEM((ROWS, COLS), F32),
            pltpu.VMEM((1, KSEL), jnp.int32),
            pltpu.VMEM((1, 1), jnp.int32),
            pltpu.VMEM((NP, 8, W, ROWS), BF16),
            pltpu.VMEM((NP, 4, W, ROWS), BF16),
            pltpu.VMEM((NP, 6, HALF, ROWS), BF16),
            pltpu.VMEM((NP, 3, W, ROWS), BF16),
            pltpu.VMEM((ROWS, W), F32),
            pltpu.VMEM((NP, ROWS, W), F32),
            pltpu.VMEM((NP, ROWS, W), BF16),
            pltpu.VMEM((NP, NY - 1, YR, W), BF16),
            pltpu.VMEM((NP, YR, W), BF16),
            pltpu.VMEM((NP, NZ - 1, ZR, W), BF16),
            pltpu.VMEM((NP, ROWS, W), BF16),
            pltpu.VMEM((TOK, COLS), F32),
            pltpu.VMEM((TOK, COLS), BF16),
            pltpu.VMEM((NP, ROWS, W), F32),
            pltpu.VMEM((NP, ROWS, W), F32),
            pltpu.VMEM((NP, ROWS, W), F32),
            dma((17,)),
            dma((7,)),
            dma((NP, 4)),
            dma((NP, 4)),
            dma((NP, 6)),
            dma((NP, 6)),
            dma((6,)),
            dma((6,)),
            dma((7,)),
            dma((7,)),
            dma((NP, NY - 1)),
            dma((NP, NY - 1)),
            dma((NP, NZ - 1)),
            dma((NP, NZ - 1)),
            dma((NP, NZ - 1)),
            dma((NP, NZ - 1)),
            dma((NP, NY - 1)),
            dma((NP, NY - 1)),
        ],
        compiler_params=pltpu.CompilerParams(
            collective_id=0, has_side_effects=True, vmem_limit_bytes=50 * 1024 * 1024
        ),
        cost_estimate=pl.CostEstimate(flops=4 * TOK * D * COLS, bytes_accessed=14 * 2**20, transcendentals=0),
    )(
        tokens, cotangent, inner_params, first_moment, second_moment, anchor, feedback, momentum,
        sel_blocks.reshape(1, KSEL), sel_count.reshape(1, 1),
    )


def solution(mesh):
    placed = (
        P(("rep", "fsdp"), None),
        P(("rep", "fsdp"), None),
        P("rep", "fsdp", None),
        P("rep", "fsdp", None),
        P("rep", "fsdp", None),
        P("fsdp", None),
        P("rep", "fsdp", None),
        P("fsdp", None),
        P("rep", "fsdp", None),
        P("rep", "fsdp"),
    )
    return jax.shard_map(
        shards,
        mesh=mesh,
        in_specs=placed,
        out_specs=(
            P(("rep", "fsdp"), None),
            P("fsdp", None),
            P("rep", "fsdp", None),
            P("fsdp", None),
        ),
        check_vma=False,
    )
```

time: 251 us -> 70.7 us (0.28)
  waiting for transfers between devices: 130 us -> 0 us
  Pallas kernels: 0 us -> 62.7 us
  other arithmetic: 53.1 us -> 0 us
  blocking collectives: 36.8 us -> 0 us
  between operations: 14.5 us -> 1.31 us
  matrix products: 13.1 us -> 0 us
  local copies, waits for them, and re-layouts: 3.3 us -> 6.46 us
    all_gather x2 -> x0, waiting for transfers between devices: 90.6 us -> none  [the longest x1 90.5 us: shards(): lax.all_gather(picked, 'rep', axis=0, tiled=True)]
    pallas_call x0 -> x1, Pallas kernels: none -> 62.7 us  [shards(): pl.pallas_call(kernel, out_shape=(jax.ShapeDtypeStruct((TOK, COLS), BF16)...]
    scatter-add x1 -> x0, other arithmetic: 44.8 us -> none  [shards(): jnp.zeros((block_count, BLK), jnp.float32).at[every_index].add(every_tile)]
    reduce_scatter x1 -> x0, waiting for transfers between devices: 38.8 us -> none  [shards(): lax.psum_scatter((lax.dot_general(inputs, cotangent, (((0,), (0,)), ((),...]
    all_gather x1 -> x0, blocking collectives: 36.8 us -> none  [shards(): lax.all_gather(chosen, 'rep', axis=0, tiled=True)]
    dot_general x2 -> x0, matrix products: 13.1 us -> none  [the longest x1 6.59 us: shards(): jnp.dot(inputs, lax.all_gather(weights, 'fsdp', axis=0, tiled=True), pref...]
    unnamed x8 -> x12, local copies, waits for them, and re-layouts: 1.01 us -> 6.46 us
    select_n x4 -> x0, other arithmetic: 4.73 us -> none  [the longest x1 3.91 us: shards(): jnp.where(marked[:, None], 0.0, block_view).reshape(shard_rows, columns)]
  transfers between devices with their start and end apart: 3 -> 0, of which waited for: 2 -> 0; matrix products, arithmetic and copies ran while one was open for 5% -> 0% of each run, Pallas kernels for 0% -> 0%
where the time goes in v1:
time: 70.7 us; the launch traced here: 70.5 us
  Pallas kernels  62.7 us (89%)
  local copies, waits for them, and re-layouts  6.46 us (9%)
  between operations  1.31 us (2%)
    pallas_call x1, Pallas kernels, shards(): pl.pallas_call(kernel, out_shape=(jax.ShapeDtypeStruct((TOK, COLS), BF16)...  62.7 us
    unnamed x12, local copies, waits for them, and re-layouts  6.46 us

profile of v1, /device:TPU:1, one launch (start us, length us, event | category | flops | bytes accessed | tf_op | source)
XLA Modules:
  0.0 70.5 jit_solution(14685155379281808449)
XLA Ops:
  1.3 0.0 copy-start
  1.3 1.0 %copy-done = bf16[512,512]{1,0:T(8,128)(2,1)S(1)} copy-done((bf16[512,512]{1,0:T(8,128)(2,1)S(1)}, bf16[512,512]{1,0:T(8,128)(2,1)}, u32[]{:S(2)}) %copy-start) | copy-done | bytes 524312
  2.3 0.0 copy-start.1
  2.3 1.0 %copy-done.1 = bf16[1,512,512]{2,1,0:T(8,128)(2,1)S(1)} copy-done((bf16[1,512,512]{2,1,0:T(8,128)(2,1)S(1)}, bf16[1,512,512]{2,1,0:T(8,128)(2,1)}, u32[]{:S(2)}) %copy-start.1) | copy-done | bytes 524312
  3.4 0.0 copy-start.2
  3.4 0.7 copy-done.2
  4.0 62.7 %shard_map.129 = (bf16[512,512]{1,0:T(8,128)(2,1)S(1)}, f32[512,512]{1,0:T(8,128)S(1)}, f32[1,512,512]{2,1,0:T(8,128)S(1)}, f32[512,512]{1,0:T(8,128)}) custom-call(bf16[512,4096]{1,0:T(8,128)(2,1)} %tok_hbm.1, bf16[512,512]{1,0:T(8,128)(2,1)S(1)} %copy-done, bf16[1,512,512]{2,1,0:T(8,128)(2,1)S(1)} %copy-done.1, f32[1,512,512]{2,1,0:T(8,128)} %first_hbm.1, ...), custom_call_target="tpu_custom_call" | custom-call | flops 4294967296 | bytes 14680064 | tf_op jit(solution)/shard_map/pallas_call | solution.py:387
  66.8 0.0 copy-start.3
  66.8 0.8 %copy.19 = bf16[512,512]{1,0:T(8,128)(2,1)} copy(bf16[512,512]{1,0:T(8,128)(2,1)S(1)} %get-tuple-element.8) | data formatting | bytes 1048576
  67.6 1.0 %copy.20 = f32[512,512]{1,0:T(8,128)} copy(f32[512,512]{1,0:T(8,128)S(1)} %get-tuple-element.9) | data formatting | bytes 2097152
  68.5 1.0 %copy.21 = f32[1,512,512]{2,1,0:T(8,128)} copy(f32[1,512,512]{2,1,0:T(8,128)S(1)} %get-tuple-element.10) | data formatting | bytes 2097152
  69.5 0.0 copy-done.3
  69.5 1.0 %copy.22 = f32[512,512]{1,0:T(8,128)} copy(f32[512,512]{1,0:T(8,128)S(1)} %copy-done.3) | data formatting | bytes 2097152
Async XLA Ops:
  1.3 1.0 %copy-start = (bf16[512,512]{1,0:T(8,128)(2,1)S(1)}, bf16[512,512]{1,0:T(8,128)(2,1)}, u32[]{:S(2)}) copy-start(bf16[512,512]{1,0:T(8,128)(2,1)} %cot_hbm.1) | copy-start | bytes 1572868
  2.3 1.0 %copy-start.1 = (bf16[1,512,512]{2,1,0:T(8,128)(2,1)S(1)}, bf16[1,512,512]{2,1,0:T(8,128)(2,1)}, u32[]{:S(2)}) copy-start(bf16[1,512,512]{2,1,0:T(8,128)(2,1)} %par_hbm.1) | copy-start | bytes 1572868
  3.4 0.7 copy-start.2
  66.8 2.7 %copy-start.3 = (f32[512,512]{1,0:T(8,128)S(1)}, f32[512,512]{1,0:T(8,128)}, u32[]{:S(2)}) copy-start(f32[512,512]{1,0:T(8,128)} %get-tuple-element.11) | copy-start | bytes 3145732

commit v2 on v1

--- a/solution.py
+++ b/solution.py
@@ -16,8 +16,9 @@
 NX = 4
 NY = 4
 NZ = 8
-NP = 2
+NP = 4
 W = COLS // NP
+PW = 256
 HALF = W // 2
 YR = ROWS // NY
 ZR = YR // NZ
@@ -41,7 +42,7 @@
     tok_hbm, cot_hbm, par_hbm, first_hbm, second_hbm, anchor_hbm, feed_hbm, mom_hbm, sel_hbm, cnt_hbm,
     key_hbm, anchor_out, feed_out, mom_out,
     tok, cot, cot_t, wts, first, second, anchor, feed, mom, sel, cnt,
-    part, sib_in, msg, fin, grad_t, mark, outg, ybuf, zsrc, zbuf, avg,
+    part, sib_in, msg, fin, mark, outg, ybuf, zsrc, zbuf, avg,
     acc, key_v, anchor_v, feed_v, mom_v,
     load_sem, store_sem,
     sib_s, sib_r, x_s, x_r, ag_s, ag_r, rel_s, rel_r,
@@ -105,20 +106,24 @@
     l_w.wait()
     pl.semaphore_wait(barrier, len(peers))
 
-    def ag(n, src_slot, rows, dst_slot, k):
+    ags = []
+
+    def ag(src_slot, dst_slot, rows, size, k):
+        n = len(ags)
         c = remote(
-            wts.at[src_slot, pl.ds(rows, 256)], wts.at[dst_slot, pl.ds(rows, 256)], ag_s.at[n], ag_r.at[n], on_x(k)
+            wts.at[src_slot, pl.ds(rows, size)], wts.at[dst_slot, pl.ds(rows, size)], ag_s.at[n], ag_r.at[n], on_x(k)
         )
         c.start()
+        ags.append(c)
         return c
 
-    ag_plus_a = ag(0, 7, 0, 5, 1)
-    ag_minus_b = ag(1, 7, 256, 3, 3)
+    plus = [ag(7, 5, 0, 128, 1)]
+    minus = [ag(7, 3, 256, 128, 3)]
 
     def products(h):
         def body(i, _):
             p = lax.dot_general(
-                cot_t[h * W : (h + 1) * W, :], tok[i], (((1,), (0,)), ((), ())), preferred_element_type=F32
+                cot_t[h * PW : (h + 1) * PW, :], tok[i], (((1,), (0,)), ((), ())), preferred_element_type=F32
             )
             part[h, i] = (p * (1.0 / math.sqrt(D))).astype(BF16)
             return 0
@@ -140,20 +145,24 @@
         return c
 
     def pair_sum(h, i, rows):
-        return part[h, 2 * i + 1, rows : rows + HALF, :].astype(F32) + sib_in[h, i, rows : rows + HALF, :].astype(F32)
+        s = slice(h % 2 * W + rows, h % 2 * W + rows + HALF)
+        return part[h // 2, 2 * i + 1, s, :].astype(F32) + sib_in[h // 2, i, s, :].astype(F32)
 
     A, B = 0, HALF
 
     def x_first(h, sib_c):
-        sib_c[0].wait_recv()
+        if h % 2 == 0:
+            sib_c[0].wait_recv()
         msg[h, 0] = pair_sum(h, 0, A).astype(BF16)
         c0 = x_send(h, 0, msg.at[h, 0], fin.at[h, 0, pl.ds(A, HALF)], 1)
         msg[h, 1] = pair_sum(h, 0, B).astype(BF16)
         c1 = x_send(h, 1, msg.at[h, 1], fin.at[h, 0, pl.ds(B, HALF)], 3)
-        sib_c[1].wait_recv()
+        if h % 2 == 0:
+            sib_c[1].wait_recv()
         msg[h, 2] = pair_sum(h, 1, B).astype(BF16)
         c2 = x_send(h, 2, msg.at[h, 2], fin.at[h, 1, pl.ds(B, HALF)], 1)
-        sib_c[2].wait_recv()
+        if h % 2 == 0:
+            sib_c[2].wait_recv()
         msg[h, 3] = pair_sum(h, 2, A).astype(BF16)
         c3 = x_send(h, 3, msg.at[h, 3], fin.at[h, 2, pl.ds(A, HALF)], 3)
         return [c0, c1, c2, c3]
@@ -173,11 +182,11 @@
         place = lax.broadcasted_iota(jnp.int32, (1, KSEL), 1)
         names = jnp.where(place < cnt[...], sel[...], -1)
         ones = jnp.ones((KSEL, W), BF16)
-        for h in range(NP):
+        for b in range(COLS // BLK):
             for r in range(0, ROWS, 128):
-                block = (lax.broadcasted_iota(jnp.int32, (128, KSEL), 0) + r) * NP + h
+                block = (lax.broadcasted_iota(jnp.int32, (128, KSEL), 0) + r) * (COLS // BLK) + b
                 hit = jnp.where(block == names, 1.0, 0.0).astype(BF16)
-                mark[h, r : r + 128, :] = jnp.dot(hit, ones, preferred_element_type=F32)
+                mark[b, r : r + 128, :] = jnp.dot(hit, ones, preferred_element_type=F32)
 
     def store(src, dst):
         c = pltpu.make_async_copy(src, dst, store_sem.at[len(stores)])
@@ -187,35 +196,36 @@
     stores = []
 
     def adam(h, sib_c, c):
-        sib_c[3].wait_recv()
+        if h % 2 == 0:
+            sib_c[3].wait_recv()
         for n in (2, 3, 4, 5):
             c[n].wait_recv()
         cols = slice(h * W, (h + 1) * W)
-
-        for d in range(0, ROWS, 128):
-            s = slice(d, d + 128)
+        half = slice(h % 2 * W, h % 2 * W + W)
+
+        def body(n, _):
+            s = pl.ds(pl.multiple_of(n * 128, 128), 128)
             total = (
-                part[h, 7, :, s].astype(F32) + sib_in[h, 3, :, s].astype(F32)
+                part[h // 2, 7, half, s].astype(F32) + sib_in[h // 2, 3, half, s].astype(F32)
                 + fin[h, 1, :, s].astype(F32) + fin[h, 2, :, s].astype(F32)
             )
-            grad_t[s, :] = jnp.transpose(total, (1, 0))
-
-        def body(n, _):
-            s = pl.ds(pl.multiple_of(n * 32, 32), 32)
-            g = grad_t[s, :]
-            first_new = beta_first * first[s, cols] + (1.0 - beta_first) * g
-            second_new = beta_second * second[s, cols] + (1.0 - beta_second) * g * g
-            master = wts[7, s, cols].astype(F32)
-            stepped = master - inner_rate * (
-                first_new / (jnp.sqrt(second_new) + epsilon) + decay_rate * master
-            )
-            combined = feed[s, cols] + (anchor[s, cols] - stepped)
-            marked = mark[h, s, :] > 0.5
-            feed_v[h, s, :] = jnp.where(marked, 0.0, combined)
-            outg[h, s, :] = jnp.where(marked, combined, 0.0).astype(BF16)
+            gradient = jnp.transpose(total, (1, 0))
+            for r in range(0, 128, 32):
+                s = pl.ds(pl.multiple_of(n * 128 + r, 32), 32)
+                g = gradient[r : r + 32, :]
+                first_new = beta_first * first[s, cols] + (1.0 - beta_first) * g
+                second_new = beta_second * second[s, cols] + (1.0 - beta_second) * g * g
+                master = wts[7, s, cols].astype(F32)
+                stepped = master - inner_rate * (
+                    first_new / (jnp.sqrt(second_new) + epsilon) + decay_rate * master
+                )
+                combined = feed[s, cols] + (anchor[s, cols] - stepped)
+                marked = mark[h * W // BLK, s, :] > 0.5
+                feed_v[h, s, :] = jnp.where(marked, 0.0, combined)
+                outg[h, s, :] = jnp.where(marked, combined, 0.0).astype(BF16)
             return 0
 
-        lax.fori_loop(0, ROWS // 32, body, 0)
+        lax.fori_loop(0, ROWS // 128, body, 0)
         store(feed_v.at[h], feed_out.at[0, :, pl.ds(h * W, W)])
         copies = []
         for k in range(1, NY):
@@ -289,84 +299,106 @@
         store(mom_v.at[h], mom_out.at[:, pl.ds(h * W, W)])
         store(anchor_v.at[h], anchor_out.at[:, pl.ds(h * W, W)])
 
-    def key_block(slot, rows, size, begin=False):
-        def body(n, _):
-            s = pl.ds(pl.multiple_of(n * 128, 128), 128)
-            p = jnp.dot(
-                tok[slot, s, rows : rows + size], wts[slot, rows : rows + size, :], preferred_element_type=F32
-            )
-            acc[s, :] = p if begin else acc[s, :] + p
-            return 0
-
-        lax.fori_loop(0, TOK // 128, body, 0)
-
-    def relay(n, slot, rows, size):
+    def key_block(slots, begin=False):
+        p = None if begin else acc[...]
+        for slot in slots:
+            q = jnp.dot(tok[slot], wts[slot], preferred_element_type=F32)
+            p = q if p is None else p + q
+        acc[...] = p
+
+    rel = []
+
+    def relay(slot, rows, size):
+        n = len(rel)
         c = remote(
             wts.at[slot, pl.ds(rows, size)], wts.at[slot - 1, pl.ds(rows, size)], rel_s.at[n], rel_r.at[n], sib
         )
         c.start()
-        return c
-
-    sib0 = products(0)
-    x0 = x_first(0, sib0)
-    sib1 = products(1)
-    x0 = x_second(0, x0)
-    x1 = x_first(1, sib1)
-    rel = [relay(0, 7, 0, ROWS)]
+        rel.append(c)
+
+    xs, ys, zs, gzs, gys = [None] * NP, [None] * NP, [None] * NP, [None] * NP, [None] * NP
+    sibs = [products(0)]
+    xs[0] = x_first(0, sibs[0])
+    xs[1] = x_first(1, sibs[0])
+    sibs.append(products(1))
+    xs[0] = x_second(0, xs[0])
+    xs[2] = x_first(2, sibs[1])
+    relay(7, 0, ROWS)
     marks()
     for one in l_state:
         one.wait()
-    key_block(7, 0, ROWS, begin=True)
-    y0 = adam(0, sib0, x0)
-    x1 = x_second(1, x1)
-
-    ag_plus_b = ag(2, 7, 256, 5, 1)
-    ag_minus_a = ag(3, 7, 0, 3, 3)
-    ag_plus_a.wait_recv()
-    ag_plus_f = ag(4, 5, 0, 1, 1)
-    rel.append(relay(1, 5, 0, 256))
-    ag_minus_b.wait_recv()
-    ag_minus_f = ag(5, 3, 256, 1, 3)
-    rel.append(relay(2, 3, 256, 256))
-
-    z0 = sync_z(0, y0)
-    y1 = adam(1, sib1, x1)
-    gz0 = gather_z(0, z0)
+    xs[1] = x_second(1, xs[1])
+    xs[3] = x_first(3, sibs[1])
+    ys[0] = adam(0, sibs[0], xs[0])
+    xs[2] = x_second(2, xs[2])
     rel[0].wait_recv()
-    key_block(6, 0, ROWS)
-    z1 = sync_z(1, y1)
-    gy0 = gather_y(0, gz0)
-    gz1 = gather_z(1, z1)
-    outer(0, gy0)
-    gy1 = gather_y(1, gz1)
-    ag_plus_b.wait_recv()
-    rel.append(relay(3, 5, 256, 256))
-    ag_minus_a.wait_recv()
-    rel.append(relay(4, 3, 0, 256))
-    key_block(5, 0, ROWS)
-    key_block(3, 0, ROWS)
-    outer(1, gy1)
-    ag_plus_f.wait_recv()
-    rel.append(relay(5, 1, 0, 256))
-    ag_minus_f.wait_recv()
-    rel.append(relay(6, 1, 256, 256))
-    key_block(1, 0, ROWS)
-    for n in (1, 3):
-        rel[n].wait_recv()
-    key_block(4, 0, ROWS)
+    key_block((7, 6), begin=True)
+    ys[1] = adam(1, sibs[0], xs[1])
+    zs[0] = sync_z(0, ys[0])
+    xs[3] = x_second(3, xs[3])
+    ys[2] = adam(2, sibs[1], xs[2])
+    zs[1] = sync_z(1, ys[1])
+    gzs[0] = gather_z(0, zs[0])
+    ys[3] = adam(3, sibs[1], xs[3])
+
+    plus[0].wait_recv()
+    minus[0].wait_recv()
+    plus += [ag(7, 5, 128, 128, 1), ag(5, 1, 0, 128, 1), ag(7, 5, 256, 256, 1)]
+    minus += [ag(7, 3, 384, 128, 3), ag(3, 1, 256, 128, 3), ag(7, 3, 0, 256, 3)]
+    relay(5, 0, 128)
+    relay(3, 256, 128)
+
+    zs[2] = sync_z(2, ys[2])
+    gzs[1] = gather_z(1, zs[1])
+    gys[0] = gather_y(0, gzs[0])
+    zs[3] = sync_z(3, ys[3])
+    plus[1].wait_recv()
+    minus[1].wait_recv()
+    plus += [ag(5, 1, 128, 128, 1)]
+    minus += [ag(3, 1, 384, 128, 3)]
+    relay(5, 128, 128)
+    relay(3, 384, 128)
+    gzs[2] = gather_z(2, zs[2])
+    gys[1] = gather_y(1, gzs[1])
+    outer(0, gys[0])
+    gzs[3] = gather_z(3, zs[3])
+    gys[2] = gather_y(2, gzs[2])
+    outer(1, gys[1])
+    gys[3] = gather_y(3, gzs[3])
+    plus[3].wait_recv()
+    relay(5, 256, 256)
+    minus[3].wait_recv()
+    relay(3, 0, 256)
+    key_block((5, 3))
+    outer(2, gys[2])
     for n in (2, 4):
-        rel[n].wait_recv()
-    key_block(2, 0, ROWS)
-    for n in (5, 6):
-        rel[n].wait_recv()
-    key_block(0, 0, ROWS)
+        plus[n].wait_recv()
+        minus[n].wait_recv()
+    relay(1, 0, 256)
+    relay(1, 256, 256)
+    outer(3, gys[3])
+    for one in rel[1:7]:
+        one.wait_recv()
+    key_block((1, 4, 2))
+    for one in rel[7:]:
+        one.wait_recv()
+    key_block((0,))
     key_v[...] = (acc[...] * (1.0 / math.sqrt(D))).astype(BF16)
     store(key_v, key_hbm)
 
-    ags = [ag_plus_a, ag_minus_b, ag_plus_b, ag_minus_a, ag_plus_f, ag_minus_f]
-    for one in sib0 + sib1 + x0 + x1 + y0 + y1 + z0 + z1 + gz0 + gz1 + gy0 + gy1 + ags + rel:
-        one.wait_send()
+    for group in sibs + xs + ys + zs + gzs + gys + [ags, rel]:
+        for one in group:
+            one.wait_send()
     for one in stores:
+        one.wait()
+
+
+def flush(*refs):
+    sem = refs[-1]
+    copies = [pltpu.make_async_copy(refs[n], refs[4 + n], sem.at[n]) for n in range(4)]
+    for one in copies:
+        one.start()
+    for one in copies:
         one.wait()
 
 
@@ -384,15 +416,17 @@
 ):
     dma = pltpu.SemaphoreType.DMA
     any_space = pl.BlockSpec(memory_space=pl.ANY)
-    return pl.pallas_call(
-        kernel,
-        out_shape=(
+    hbm = pl.BlockSpec(memory_space=pltpu.HBM)
+    outs = (
             jax.ShapeDtypeStruct((TOK, COLS), BF16),
             jax.ShapeDtypeStruct((ROWS, COLS), F32),
             jax.ShapeDtypeStruct((1, ROWS, COLS), F32),
             jax.ShapeDtypeStruct((ROWS, COLS), F32),
-        ),
-        in_specs=[any_space] * 10,
+        )
+    done = pl.pallas_call(
+        kernel,
+        out_shape=outs,
+        in_specs=[hbm] * 10,
         out_specs=(any_space,) * 4,
         scratch_shapes=[
             pltpu.VMEM((8, TOK, ROWS), BF16),
@@ -406,12 +440,11 @@
             pltpu.VMEM((ROWS, COLS), F32),
             pltpu.VMEM((1, KSEL), jnp.int32),
             pltpu.VMEM((1, 1), jnp.int32),
-            pltpu.VMEM((NP, 8, W, ROWS), BF16),
-            pltpu.VMEM((NP, 4, W, ROWS), BF16),
+            pltpu.VMEM((COLS // PW, 8, PW, ROWS), BF16),
+            pltpu.VMEM((COLS // PW, 4, PW, ROWS), BF16),
             pltpu.VMEM((NP, 6, HALF, ROWS), BF16),
             pltpu.VMEM((NP, 3, W, ROWS), BF16),
-            pltpu.VMEM((ROWS, W), F32),
-            pltpu.VMEM((NP, ROWS, W), F32),
+            pltpu.VMEM((COLS // BLK, ROWS, W), F32),
             pltpu.VMEM((NP, ROWS, W), BF16),
             pltpu.VMEM((NP, NY - 1, YR, W), BF16),
             pltpu.VMEM((NP, YR, W), BF16),
@@ -423,15 +456,15 @@
             pltpu.VMEM((NP, ROWS, W), F32),
             pltpu.VMEM((NP, ROWS, W), F32),
             dma((17,)),
-            dma((7,)),
-            dma((NP, 4)),
-            dma((NP, 4)),
+            dma((3 * NP + 1,)),
+            dma((COLS // PW, 4)),
+            dma((COLS // PW, 4)),
             dma((NP, 6)),
             dma((NP, 6)),
-            dma((6,)),
-            dma((6,)),
-            dma((7,)),
-            dma((7,)),
+            dma((10,)),
+            dma((10,)),
+            dma((11,)),
+            dma((11,)),
             dma((NP, NY - 1)),
             dma((NP, NY - 1)),
             dma((NP, NZ - 1)),
@@ -442,13 +475,27 @@
             dma((NP, NY - 1)),
         ],
         compiler_params=pltpu.CompilerParams(
-            collective_id=0, has_side_effects=True, vmem_limit_bytes=50 * 1024 * 1024
+            collective_id=0, has_side_effects=True, vmem_limit_bytes=40 * 1024 * 1024
         ),
         cost_estimate=pl.CostEstimate(flops=4 * TOK * D * COLS, bytes_accessed=14 * 2**20, transcendentals=0),
     )(
-        tokens, cotangent, inner_params, first_moment, second_moment, anchor, feedback, momentum,
-        sel_blocks.reshape(1, KSEL), sel_count.reshape(1, 1),
+        *(
+            pltpu.with_memory_space_constraint(a, pltpu.HBM)
+            for a in (
+                tokens, cotangent, inner_params, first_moment, second_moment, anchor, feedback, momentum,
+                sel_blocks.reshape(1, KSEL),
+            )
+        ),
+        sel_count.reshape(1, 1),
     )
+    return pl.pallas_call(
+        flush,
+        out_shape=outs,
+        in_specs=[any_space] * 4,
+        out_specs=(any_space,) * 4,
+        scratch_shapes=[dma((4,))],
+        compiler_params=pltpu.CompilerParams(has_side_effects=True, vmem_limit_bytes=4 * 1024 * 1024),
+    )(*done)
 
 
 def solution(mesh):

time: 70.7 us -> 58.3 us (0.82)
  local copies, waits for them, and re-layouts: 6.46 us -> 0 us
  Pallas kernels: 62.7 us -> 56.9 us
    unnamed x12 -> x0, local copies, waits for them, and re-layouts: 6.46 us -> none
    pallas_call x1 -> x2, Pallas kernels: 62.7 us -> 56.9 us  [the longest x1 55.1 us: shards(): pl.pallas_call(kernel, out_shape=outs, in_specs=[hbm] * 10, out_specs=(an...]
where the time goes in v2:
time: 58.3 us; the launch traced here: 58.2 us
  Pallas kernels  56.9 us (98%)
  between operations  1.29 us (2%)
    pallas_call x1, Pallas kernels, shards(): pl.pallas_call(kernel, out_shape=outs, in_specs=[hbm] * 10, out_specs=(an...  55.1 us
    pallas_call x1, Pallas kernels, shards(): pl.pallas_call(flush, out_shape=outs, in_specs=[any_space] * 4, out_specs...  1.87 us

profile of v2, /device:TPU:1, one launch (start us, length us, event | category | flops | bytes accessed | tf_op | source)
XLA Modules:
  0.0 58.2 jit_solution(9269594591227487106)
XLA Ops:
  1.3 55.1 %shard_map.129 = (bf16[512,512]{1,0:T(8,128)(2,1)S(1)}, f32[512,512]{1,0:T(8,128)S(1)}, f32[1,512,512]{2,1,0:T(8,128)S(1)}, f32[512,512]{1,0:T(8,128)S(1)}) custom-call(bf16[512,4096]{1,0:T(8,128)(2,1)} %tok_hbm.1, bf16[512,512]{1,0:T(8,128)(2,1)} %cot_hbm.1, bf16[1,512,512]{2,1,0:T(8,128)(2,1)} %par_hbm.1, f32[1,512,512]{2,1,0:T(8,128)} %first_hbm.1, ...), custom_call_target="tpu_custom_call" | custom-call | flops 4294967296 | bytes 14680064 | tf_op jit(solution)/shard_map/pallas_call | solution.py:426
  56.3 1.9 %shard_map.130 = (bf16[512,512]{1,0:T(8,128)(2,1)}, f32[512,512]{1,0:T(8,128)}, f32[1,512,512]{2,1,0:T(8,128)}, f32[512,512]{1,0:T(8,128)}) custom-call(bf16[512,512]{1,0:T(8,128)(2,1)S(1)} %get-tuple-element.8.refs_0_, f32[512,512]{1,0:T(8,128)S(1)} %get-tuple-element.9.refs_1_, f32[1,512,512]{2,1,0:T(8,128)S(1)} %get-tuple-element.10.refs_2_, ...), custom_call_target="tpu_custom_call" | custom-call | tf_op jit(solution)/shard_map/pallas_call | solution.py:491

commit v3 on v2

--- a/solution.py
+++ b/solution.py
@@ -36,6 +36,7 @@
 BF16 = jnp.bfloat16
 
 ORDER = (2, 1, 3, 0)
+FAR_FIRST = (4, 3, 5, 2, 6, 1, 7)
 
 
 def kernel(
@@ -79,13 +80,21 @@
         c.start()
         return c
 
-    l_cot = load(cot_hbm, cot)
-    l_w = load(par_hbm.at[0], wts.at[7])
-    l_tok = []
-    for i in range(8):
+    def load_tok(i):
         chip = lax.rem(x + ORDER[i // 2], NX)
         shard = chip * 2 + (1 - core if i % 2 == 0 else core)
-        l_tok.append(load(tok_hbm.at[:, pl.ds(pl.multiple_of(shard * ROWS, ROWS), ROWS)], tok.at[i]))
+        return load(tok_hbm.at[:, pl.ds(pl.multiple_of(shard * ROWS, ROWS), ROWS)], tok.at[i])
+
+    l_cot = load(cot_hbm, cot)
+    l_tok = [load_tok(0), load_tok(1)]
+
+    barrier = pltpu.get_barrier_semaphore()
+    peers = [sib, on_x(1), on_x(3)] + [on_y(k) for k in range(1, NY)] + [on_z(k) for k in range(1, NZ)]
+    for dev in peers:
+        pl.semaphore_signal(barrier, inc=1, device_id=dev, device_id_type=MESH)
+
+    l_w = load(par_hbm.at[0], wts.at[7])
+    l_tok += [load_tok(i) for i in range(2, 8)]
     l_sel = load(sel_hbm, sel)
     l_cnt = load(cnt_hbm, cnt)
     l_state = [
@@ -95,16 +104,8 @@
         load(feed_hbm.at[0], feed),
         load(mom_hbm, mom),
     ]
-
-    barrier = pltpu.get_barrier_semaphore()
-    peers = [sib, on_x(1), on_x(3)] + [on_y(k) for k in range(1, NY)] + [on_z(k) for k in range(1, NZ)]
-    for dev in peers:
-        pl.semaphore_signal(barrier, inc=1, device_id=dev, device_id_type=MESH)
-
     l_cot.wait()
     cot_t[...] = jnp.transpose(cot[...], (1, 0))
-    l_w.wait()
-    pl.semaphore_wait(barrier, len(peers))
 
     ags = []
 
@@ -117,27 +118,19 @@
         ags.append(c)
         return c
 
-    plus = [ag(7, 5, 0, 128, 1)]
-    minus = [ag(7, 3, 256, 128, 3)]
-
-    def products(h):
-        def body(i, _):
-            p = lax.dot_general(
-                cot_t[h * PW : (h + 1) * PW, :], tok[i], (((1,), (0,)), ((), ())), preferred_element_type=F32
-            )
-            part[h, i] = (p * (1.0 / math.sqrt(D))).astype(BF16)
-            return 0
-
-        copies = []
-        for i in range(8):
-            if h == 0:
-                l_tok[i].wait()
-            body(i, 0)
-            if i % 2 == 0:
-                c = remote(part.at[h, i], sib_in.at[h, i // 2], sib_s.at[h, i // 2], sib_r.at[h, i // 2], sib)
-                c.start()
-                copies.append(c)
-        return copies
+    def product(i):
+        l_tok[i].wait()
+        p = jnp.dot(cot_t[...], tok[i], preferred_element_type=F32)
+        p = (p * (1.0 / math.sqrt(D))).astype(BF16)
+        for h in range(COLS // PW):
+            part[h, i] = p[h * PW : (h + 1) * PW, :]
+
+    sibs = [[], []]
+
+    def exchange(h, i):
+        c = remote(part.at[h, 2 * i], sib_in.at[h, i], sib_s.at[h, i], sib_r.at[h, i], sib)
+        c.start()
+        sibs[h].append(c)
 
     def x_send(h, n, src, dst, k):
         c = remote(src, dst, x_s.at[h, n], x_r.at[h, n], on_x(k))
@@ -150,31 +143,29 @@
 
     A, B = 0, HALF
 
-    def x_first(h, sib_c):
-        if h % 2 == 0:
-            sib_c[0].wait_recv()
+    xs = [[] for _ in range(NP)]
+
+    def x_first(h):
         msg[h, 0] = pair_sum(h, 0, A).astype(BF16)
-        c0 = x_send(h, 0, msg.at[h, 0], fin.at[h, 0, pl.ds(A, HALF)], 1)
+        xs[h].append(x_send(h, 0, msg.at[h, 0], fin.at[h, 0, pl.ds(A, HALF)], 1))
         msg[h, 1] = pair_sum(h, 0, B).astype(BF16)
-        c1 = x_send(h, 1, msg.at[h, 1], fin.at[h, 0, pl.ds(B, HALF)], 3)
-        if h % 2 == 0:
-            sib_c[1].wait_recv()
+        xs[h].append(x_send(h, 1, msg.at[h, 1], fin.at[h, 0, pl.ds(B, HALF)], 3))
+
+    def x_plus(h):
         msg[h, 2] = pair_sum(h, 1, B).astype(BF16)
-        c2 = x_send(h, 2, msg.at[h, 2], fin.at[h, 1, pl.ds(B, HALF)], 1)
-        if h % 2 == 0:
-            sib_c[2].wait_recv()
+        xs[h].append(x_send(h, 2, msg.at[h, 2], fin.at[h, 1, pl.ds(B, HALF)], 1))
+
+    def x_minus(h):
         msg[h, 3] = pair_sum(h, 2, A).astype(BF16)
-        c3 = x_send(h, 3, msg.at[h, 3], fin.at[h, 2, pl.ds(A, HALF)], 3)
-        return [c0, c1, c2, c3]
-
-    def x_second(h, c):
-        c[0].wait_recv()
+        xs[h].append(x_send(h, 3, msg.at[h, 3], fin.at[h, 2, pl.ds(A, HALF)], 3))
+
+    def x_second(h):
+        xs[h][0].wait_recv()
         msg[h, 4] = (pair_sum(h, 1, A) + fin[h, 0, A : A + HALF, :].astype(F32)).astype(BF16)
-        c4 = x_send(h, 4, msg.at[h, 4], fin.at[h, 1, pl.ds(A, HALF)], 1)
-        c[1].wait_recv()
+        xs[h].append(x_send(h, 4, msg.at[h, 4], fin.at[h, 1, pl.ds(A, HALF)], 1))
+        xs[h][1].wait_recv()
         msg[h, 5] = (pair_sum(h, 2, B) + fin[h, 0, B : B + HALF, :].astype(F32)).astype(BF16)
-        c5 = x_send(h, 5, msg.at[h, 5], fin.at[h, 2, pl.ds(B, HALF)], 3)
-        return c + [c4, c5]
+        xs[h].append(x_send(h, 5, msg.at[h, 5], fin.at[h, 2, pl.ds(B, HALF)], 3))
 
     def marks():
         l_sel.wait()
@@ -195,23 +186,22 @@
 
     stores = []
 
-    def adam(h, sib_c, c):
-        if h % 2 == 0:
-            sib_c[3].wait_recv()
+    def adam(h):
         for n in (2, 3, 4, 5):
-            c[n].wait_recv()
+            xs[h][n].wait_recv()
         cols = slice(h * W, (h + 1) * W)
         half = slice(h % 2 * W, h % 2 * W + W)
-
-        def body(n, _):
-            s = pl.ds(pl.multiple_of(n * 128, 128), 128)
+        copies = []
+        for k in (2, 1, 3, 0):
+            first_row = pl.multiple_of(lax.rem(y + k, NY) * YR, YR)
+            block = pl.ds(first_row, YR)
             total = (
-                part[h // 2, 7, half, s].astype(F32) + sib_in[h // 2, 3, half, s].astype(F32)
-                + fin[h, 1, :, s].astype(F32) + fin[h, 2, :, s].astype(F32)
+                part[h // 2, 7, half, block].astype(F32) + sib_in[h // 2, 3, half, block].astype(F32)
+                + fin[h, 1, :, block].astype(F32) + fin[h, 2, :, block].astype(F32)
             )
             gradient = jnp.transpose(total, (1, 0))
-            for r in range(0, 128, 32):
-                s = pl.ds(pl.multiple_of(n * 128 + r, 32), 32)
+            for r in range(0, YR, 32):
+                s = pl.ds(pl.multiple_of(first_row + r, 32), 32)
                 g = gradient[r : r + 32, :]
                 first_new = beta_first * first[s, cols] + (1.0 - beta_first) * g
                 second_new = beta_second * second[s, cols] + (1.0 - beta_second) * g * g
@@ -223,19 +213,11 @@
                 marked = mark[h * W // BLK, s, :] > 0.5
                 feed_v[h, s, :] = jnp.where(marked, 0.0, combined)
                 outg[h, s, :] = jnp.where(marked, combined, 0.0).astype(BF16)
-            return 0
-
-        lax.fori_loop(0, ROWS // 128, body, 0)
+            if k > 0:
+                c = remote(outg.at[h, block], ybuf.at[h, k - 1], y_s.at[h, k - 1], y_r.at[h, k - 1], on_y(k))
+                c.start()
+                copies.append(c)
         store(feed_v.at[h], feed_out.at[0, :, pl.ds(h * W, W)])
-        copies = []
-        for k in range(1, NY):
-            to = lax.rem(y + k, NY)
-            c = remote(
-                outg.at[h, pl.ds(pl.multiple_of(to * YR, YR), YR)], ybuf.at[h, k - 1],
-                y_s.at[h, k - 1], y_r.at[h, k - 1], on_y(k),
-            )
-            c.start()
-            copies.append(c)
         return copies
 
     def sync_z(h, c):
@@ -246,7 +228,7 @@
             total = total + ybuf[h, k].astype(F32)
         zsrc[h] = total.astype(BF16)
         copies = []
-        for k in range(1, NZ):
+        for k in FAR_FIRST:
             to = lax.rem(z + k, NZ)
             c = remote(
                 zsrc.at[h, pl.ds(pl.multiple_of(to * ZR, ZR), ZR)], zbuf.at[h, k - 1],
@@ -265,7 +247,7 @@
         mine = pl.ds(pl.multiple_of(y * YR + z * ZR, ZR), ZR)
         avg[h, mine, :] = (total * (1.0 / (NY * NZ))).astype(BF16)
         copies = []
-        for k in range(1, NZ):
+        for k in FAR_FIRST:
             c = remote(avg.at[h, mine], avg.at[h, mine], gz_s.at[h, k - 1], gz_r.at[h, k - 1], on_z(k))
             c.start()
             copies.append(c)
@@ -316,75 +298,110 @@
         c.start()
         rel.append(c)
 
-    xs, ys, zs, gzs, gys = [None] * NP, [None] * NP, [None] * NP, [None] * NP, [None] * NP
-    sibs = [products(0)]
-    xs[0] = x_first(0, sibs[0])
-    xs[1] = x_first(1, sibs[0])
-    sibs.append(products(1))
-    xs[0] = x_second(0, xs[0])
-    xs[2] = x_first(2, sibs[1])
+    ys, zs, gzs, gys = [None] * NP, [None] * NP, [None] * NP, [None] * NP
+    product(0)
+    pl.semaphore_wait(barrier, len(peers))
+    exchange(0, 0)
+    exchange(1, 0)
+    l_w.wait()
+    plus = [ag(7, 5, 0, 64, 1)]
+    minus = [ag(7, 3, 256, 64, 3)]
+    product(1)
+    product(2)
+    exchange(0, 1)
+    product(3)
+    sibs[0][0].wait_recv()
+    x_first(0)
+    x_first(1)
+    product(4)
+    exchange(0, 2)
+    exchange(1, 1)
+    exchange(1, 2)
+    sibs[1][0].wait_recv()
+    x_first(2)
+    x_first(3)
+    sibs[0][1].wait_recv()
+    x_plus(0)
+    product(5)
+    sibs[0][2].wait_recv()
+    x_minus(0)
+    x_second(0)
+    x_plus(1)
+    x_minus(1)
+    product(6)
+    exchange(0, 3)
+    exchange(1, 3)
+    x_second(1)
+    sibs[1][1].wait_recv()
+    x_plus(2)
+    sibs[1][2].wait_recv()
+    x_minus(2)
+    product(7)
+    x_second(2)
+    x_plus(3)
+    x_minus(3)
+    marks()
+    x_second(3)
     relay(7, 0, ROWS)
-    marks()
+    plus += [ag(7, 5, 64, 192, 1)]
+    minus += [ag(7, 3, 320, 192, 3)]
+    plus[0].wait_recv()
+    minus[0].wait_recv()
+    plus += [ag(5, 1, 0, 64, 1), ag(7, 5, 256, 256, 1)]
+    minus += [ag(3, 1, 256, 64, 3), ag(7, 3, 0, 256, 3)]
+    relay(5, 0, 64)
+    relay(3, 256, 64)
     for one in l_state:
         one.wait()
-    xs[1] = x_second(1, xs[1])
-    xs[3] = x_first(3, sibs[1])
-    ys[0] = adam(0, sibs[0], xs[0])
-    xs[2] = x_second(2, xs[2])
+    sibs[0][3].wait_recv()
+    ys[0] = adam(0)
     rel[0].wait_recv()
     key_block((7, 6), begin=True)
-    ys[1] = adam(1, sibs[0], xs[1])
+    ys[1] = adam(1)
     zs[0] = sync_z(0, ys[0])
-    xs[3] = x_second(3, xs[3])
-    ys[2] = adam(2, sibs[1], xs[2])
+    sibs[1][3].wait_recv()
+    ys[2] = adam(2)
     zs[1] = sync_z(1, ys[1])
-    gzs[0] = gather_z(0, zs[0])
-    ys[3] = adam(3, sibs[1], xs[3])
-
-    plus[0].wait_recv()
-    minus[0].wait_recv()
-    plus += [ag(7, 5, 128, 128, 1), ag(5, 1, 0, 128, 1), ag(7, 5, 256, 256, 1)]
-    minus += [ag(7, 3, 384, 128, 3), ag(3, 1, 256, 128, 3), ag(7, 3, 0, 256, 3)]
-    relay(5, 0, 128)
-    relay(3, 256, 128)
+    ys[3] = adam(3)
 
     zs[2] = sync_z(2, ys[2])
-    gzs[1] = gather_z(1, zs[1])
-    gys[0] = gather_y(0, gzs[0])
     zs[3] = sync_z(3, ys[3])
     plus[1].wait_recv()
+    plus.append(ag(5, 1, 64, 192, 1))
     minus[1].wait_recv()
-    plus += [ag(5, 1, 128, 128, 1)]
-    minus += [ag(3, 1, 384, 128, 3)]
-    relay(5, 128, 128)
-    relay(3, 384, 128)
+    minus.append(ag(3, 1, 320, 192, 3))
+    relay(5, 64, 192)
+    relay(3, 320, 192)
+    gzs[0] = gather_z(0, zs[0])
+    gzs[1] = gather_z(1, zs[1])
+    plus[2].wait_recv()
+    relay(1, 0, 64)
+    minus[2].wait_recv()
+    relay(1, 256, 64)
     gzs[2] = gather_z(2, zs[2])
-    gys[1] = gather_y(1, gzs[1])
-    outer(0, gys[0])
     gzs[3] = gather_z(3, zs[3])
-    gys[2] = gather_y(2, gzs[2])
-    outer(1, gys[1])
-    gys[3] = gather_y(3, gzs[3])
+    for h in range(NP - 1):
+        gys[h] = gather_y(h, gzs[h])
     plus[3].wait_recv()
     relay(5, 256, 256)
     minus[3].wait_recv()
     relay(3, 0, 256)
     key_block((5, 3))
+    gys[3] = gather_y(3, gzs[3])
+    outer(0, gys[0])
+    plus[4].wait_recv()
+    relay(1, 64, 192)
+    minus[4].wait_recv()
+    relay(1, 320, 192)
+    key_block((1,))
+    outer(1, gys[1])
     outer(2, gys[2])
-    for n in (2, 4):
-        plus[n].wait_recv()
-        minus[n].wait_recv()
-    relay(1, 0, 256)
-    relay(1, 256, 256)
-    outer(3, gys[3])
-    for one in rel[1:7]:
+    for one in rel[1:]:
         one.wait_recv()
-    key_block((1, 4, 2))
-    for one in rel[7:]:
-        one.wait_recv()
-    key_block((0,))
+    key_block((4, 2, 0))
     key_v[...] = (acc[...] * (1.0 / math.sqrt(D))).astype(BF16)
     store(key_v, key_hbm)
+    outer(3, gys[3])
 
     for group in sibs + xs + ys + zs + gzs + gys + [ags, rel]:
         for one in group:

time: 58.3 us -> 55 us (0.943)
  Pallas kernels: 56.9 us -> 53.6 us
    pallas_call x1, Pallas kernels: 55.1 us -> 51.7 us  [shards(): pl.pallas_call(kernel, out_shape=outs, in_specs=[hbm] * 10, out_specs=(an...]
where the time goes in v3:
time: 55 us; the launch traced here: 54.9 us
  Pallas kernels  53.6 us (97%)
  between operations  1.29 us (2%)
    pallas_call x1, Pallas kernels, shards(): pl.pallas_call(kernel, out_shape=outs, in_specs=[hbm] * 10, out_specs=(an...  51.7 us
    pallas_call x1, Pallas kernels, shards(): pl.pallas_call(flush, out_shape=outs, in_specs=[any_space] * 4, out_specs...  1.87 us

profile of v3, /device:TPU:1, one launch (start us, length us, event | category | flops | bytes accessed | tf_op | source)
XLA Modules:
  0.0 54.9 jit_solution(8818135068350137258)
XLA Ops:
  1.3 51.7 %shard_map.129 = (bf16[512,512]{1,0:T(8,128)(2,1)S(1)}, f32[512,512]{1,0:T(8,128)S(1)}, f32[1,512,512]{2,1,0:T(8,128)S(1)}, f32[512,512]{1,0:T(8,128)S(1)}) custom-call(bf16[512,4096]{1,0:T(8,128)(2,1)} %tok_hbm.1, bf16[512,512]{1,0:T(8,128)(2,1)} %cot_hbm.1, bf16[1,512,512]{2,1,0:T(8,128)(2,1)} %par_hbm.1, f32[1,512,512]{2,1,0:T(8,128)} %first_hbm.1, ...), custom_call_target="tpu_custom_call" | custom-call | flops 4294967296 | bytes 14680064 | tf_op jit(solution)/shard_map/pallas_call | solution.py:443
  53.0 1.9 %shard_map.130 = (bf16[512,512]{1,0:T(8,128)(2,1)}, f32[512,512]{1,0:T(8,128)}, f32[1,512,512]{2,1,0:T(8,128)}, f32[512,512]{1,0:T(8,128)}) custom-call(bf16[512,512]{1,0:T(8,128)(2,1)S(1)} %get-tuple-element.8.refs_0_, f32[512,512]{1,0:T(8,128)S(1)} %get-tuple-element.9.refs_1_, f32[1,512,512]{2,1,0:T(8,128)S(1)} %get-tuple-element.10.refs_2_, ...), custom_call_target="tpu_custom_call" | custom-call | tf_op jit(solution)/shard_map/pallas_call | solution.py:508

commit v4 on v3

--- a/solution.py
+++ b/solution.py
@@ -89,7 +89,7 @@
     l_tok = [load_tok(0), load_tok(1)]
 
     barrier = pltpu.get_barrier_semaphore()
-    peers = [sib, on_x(1), on_x(3)] + [on_y(k) for k in range(1, NY)] + [on_z(k) for k in range(1, NZ)]
+    peers = [on_z(k) for k in FAR_FIRST] + [on_y(k) for k in range(1, NY)] + [on_x(1), on_x(3), sib]
     for dev in peers:
         pl.semaphore_signal(barrier, inc=1, device_id=dev, device_id_type=MESH)
 
@@ -302,17 +302,17 @@
     product(0)
     pl.semaphore_wait(barrier, len(peers))
     exchange(0, 0)
-    exchange(1, 0)
     l_w.wait()
     plus = [ag(7, 5, 0, 64, 1)]
     minus = [ag(7, 3, 256, 64, 3)]
     product(1)
-    product(2)
-    exchange(0, 1)
-    product(3)
     sibs[0][0].wait_recv()
     x_first(0)
     x_first(1)
+    product(2)
+    exchange(0, 1)
+    exchange(1, 0)
+    product(3)
     product(4)
     exchange(0, 2)
     exchange(1, 1)

time: 55 us -> 54.7 us (level)
  no operation moved by 1% of the time
where the time goes in v4:
time: 54.7 us; the launch traced here: 54.6 us
  Pallas kernels  53.3 us (97%)
  between operations  1.29 us (2%)
    pallas_call x1, Pallas kernels, shards(): pl.pallas_call(kernel, out_shape=outs, in_specs=[hbm] * 10, out_specs=(an...  51.4 us
    pallas_call x1, Pallas kernels, shards(): pl.pallas_call(flush, out_shape=outs, in_specs=[any_space] * 4, out_specs...  1.87 us

profile of v4, /device:TPU:1, one launch (start us, length us, event | category | flops | bytes accessed | tf_op | source)
XLA Modules:
  0.0 54.6 jit_solution(12632477998047394656)
XLA Ops:
  1.3 51.4 %shard_map.129 = (bf16[512,512]{1,0:T(8,128)(2,1)S(1)}, f32[512,512]{1,0:T(8,128)S(1)}, f32[1,512,512]{2,1,0:T(8,128)S(1)}, f32[512,512]{1,0:T(8,128)S(1)}) custom-call(bf16[512,4096]{1,0:T(8,128)(2,1)} %tok_hbm.1, bf16[512,512]{1,0:T(8,128)(2,1)} %cot_hbm.1, bf16[1,512,512]{2,1,0:T(8,128)(2,1)} %par_hbm.1, f32[1,512,512]{2,1,0:T(8,128)} %first_hbm.1, ...), custom_call_target="tpu_custom_call" | custom-call | flops 4294967296 | bytes 14680064 | tf_op jit(solution)/shard_map/pallas_call | solution.py:443
  52.7 1.9 %shard_map.130 = (bf16[512,512]{1,0:T(8,128)(2,1)}, f32[512,512]{1,0:T(8,128)}, f32[1,512,512]{2,1,0:T(8,128)}, f32[512,512]{1,0:T(8,128)}) custom-call(bf16[512,512]{1,0:T(8,128)(2,1)S(1)} %get-tuple-element.8.refs_0_, f32[512,512]{1,0:T(8,128)S(1)} %get-tuple-element.9.refs_1_, f32[1,512,512]{2,1,0:T(8,128)S(1)} %get-tuple-element.10.refs_2_, ...), custom_call_target="tpu_custom_call" | custom-call | tf_op jit(solution)/shard_map/pallas_call | solution.py:508
